TPU v7x, 512 devices: a whole 4x8x8 slice. The times are simulated.
512 devices in a mesh: rx: 32 (over z, y_lo, core), freq: 16 (over y_hi, x).
Axes of the slice: x: 4, y: 8 (y_hi: 4, y_lo: 2; y = y_hi * 2 + y_lo), z: 8, core: 2. Of those that a mesh axis runs over, the one named last changes fastest.
Arguments:
- spectra: bfloat16 [2, 128, 32, 8192], P(None, 'freq', None, 'rx'), may hold values from -60 to 60
- source_block: int32 [1], replicated, may hold values from 0 to 31
Outputs:
- correlations: bfloat16 [256, 256, 8192], P(None, 'freq', 'rx')
All inputs are finite; a program needn't handle non-finite values.
Results may differ from a plain program's by a relative error of at most 0.0057.
Values may be sent and summed in bfloat16 or wider, within the bound.
A program may use at most 64 MiB of HBM per device.

v0:
```python
import math
import jax
import jax.numpy as jnp
from jax import lax
from jax.sharding import PartitionSpec as P

F = 128
W = 32
LAGS = 256


def extended(cells, sides, width):
    for axis, dim in sides:
        count = lax.axis_size(axis)
        ends = count - 1
        head = lax.slice_in_dim(cells, 0, width, axis=dim)
        tail = lax.slice_in_dim(cells, cells.shape[dim] - width, cells.shape[dim], axis=dim)
        cells = jnp.concatenate(
            [
                lax.ppermute(tail, axis, [(i, (i + 1) % count) for i in range(ends)]),
                cells,
                lax.ppermute(head, axis, [((i + 1) % count, i) for i in range(ends)]),
            ],
            axis=dim,
        )
    return cells


def broadcast(value, axis, source):
    kept = jnp.where(lax.axis_index(axis) == source, value, 0).astype(value.dtype)
    return lax.psum(kept, axis)


def whiten(planes_in):
    planes = planes_in.astype(jnp.float32)
    magnitude = jnp.sqrt(planes[0] * planes[0] + planes[1] * planes[1])
    padded = extended(magnitude, (("freq", 0),), 1)
    smooth = (padded[:-2] + padded[1:-1] + padded[2:]) / 3.0
    divisor = jnp.maximum(smooth, 0.5)
    return (planes / divisor[None]).astype(jnp.bfloat16)


def build_lag_basis():
    bins = jnp.arange(F, dtype=jnp.int32)
    lagged = jnp.arange(LAGS, dtype=jnp.int32)
    phase = bins[:, None] * lagged[None, :] % LAGS
    angle = phase.astype(jnp.float32) * (2.0 * math.pi / LAGS)
    return jnp.concatenate([jnp.cos(angle), -jnp.sin(angle)], axis=0).astype(jnp.bfloat16)


def window_products(sent, white):
    joined_sources = jnp.concatenate([sent[0], sent[1]], axis=1)
    leading_operand = jnp.concatenate([white[0], white[1]], axis=1)
    trailing_operand = jnp.concatenate([white[1], -white[0]], axis=1)
    real_total = jnp.einsum(
        "pgo,pgd->pod", joined_sources, leading_operand, preferred_element_type=jnp.float32
    )
    imaginary_total = jnp.einsum(
        "pgo,pgd->pod", joined_sources, trailing_operand, preferred_element_type=jnp.float32
    )
    return (real_total, imaginary_total)


def transform(cross_part, basis_table):
    stacked = cross_part.reshape(2 * F, cross_part.shape[2], cross_part.shape[3])
    lagged = jnp.einsum("kl,ksr->slr", basis_table, stacked, preferred_element_type=jnp.float32) * (
        2.0 / F
    )
    return lagged.astype(jnp.bfloat16)


def on_device(spectra, source_block):
    white = whiten(spectra)
    owner = source_block[0]
    sent = broadcast(white, "rx", owner)
    real_total, imaginary_total = window_products(sent, white)
    cross = (jnp.stack([real_total, imaginary_total]) / W).astype(jnp.bfloat16)
    basis_table = build_lag_basis()
    spread = lax.all_to_all(cross, "freq", split_axis=2, concat_axis=1, tiled=True)
    lagged = transform(spread, basis_table)
    result = lax.all_to_all(lagged, "freq", split_axis=1, concat_axis=0, tiled=True)
    return result


def solution(mesh):
    in_specs = (P(None, "freq", None, "rx"), P())
    out_specs = P(None, "freq", "rx")
    return jax.shard_map(
        on_device, mesh=mesh, in_specs=in_specs, out_specs=out_specs, check_vma=False
    )
```

profile of v0, /device:TPU:1, one launch (start us, length us, event | category | flops | bytes accessed | tf_op | source)
XLA Modules:
  0.0 392.1 jit_solution(4345271281972983025)
XLA Ops:
  6.5 0.0 all-reduce.2.cloned.1.call-start
  6.5 1.1 convert_element_type.23
  7.6 0.1 fusion.10
  7.7 3.9 %collective-permute-start = (f32[1,32,256]{2,1,0:T(8,128)S(1)}, f32[1,32,256]{2,1,0:T(8,128)S(1)}, u32[]{:S(2)}, u32[]{:S(2)}) collective-permute-start(f32[1,32,256]{2,1,0:T(8,128)S(1)} %get-tuple-element.11), channel_id=1, source_target_pairs={{0,1},{1,2},{2,3},{3,4},{4,5},{5,6},{6,7},{7,8},{8,9},{9,10},{10,1... | collective-permute-start | bytes 98312 | tf_op jit(solution)/shard_map/ppermute | solution.py:20
  11.7 1.3 collective-permute-start.1
  13.0 0.1 fusion.29
  13.7 0.0 collective-permute-done
  13.7 2.6 collective-permute-done.1
  16.4 0.8 broadcast_select_fusion
  17.2 0.0 all-reduce.2.cloned.1.call-update
  17.3 237.6 %all-reduce.2.cloned.1.call-done = bf16[2,8,32,256]{3,2,1,0:T(8,128)(2,1)} async-done(((bf16[2,8,32,256]{3,2,1,0:T(8,128)(2,1)}), bf16[2,8,32,256]{3,2,1,0:T(8,128)(2,1)}) %all-reduce.2.cloned.1.call-update) | async-done | bytes 262160 | tf_op jit(solution)/shard_map/psum | solution.py:31
  254.9 1.0 slice_bitcast_fusion.3
  255.8 0.5 convolution_bitcast_fusion.1
  256.3 0.5 convolution_bitcast_fusion
  256.8 0.5 fusion
  257.3 2.5 copy.17
  259.8 8.1 %all-to-all-start = ((bf16[2,8,256,256]{3,1,0,2:T(8,128)(2,1)}), bf16[2,8,256,256]{3,1,0,2:T(8,128)(2,1)S(1)}, u32[]{:S(2)}, u32[]{:S(2)}) async-start(bf16[2,8,256,256]{3,1,0,2:T(8,128)(2,1)} %copy.17), calls=%async_computation | async-start | bytes 4194304 | tf_op jit(solution)/shard_map/all_to_all | solution.py:79
  267.9 0.5 negate_convert_fusion
  268.4 52.8 %all-to-all-done = bf16[2,8,256,256]{3,1,0,2:T(8,128)(2,1)S(1)} async-done(((bf16[2,8,256,256]{3,1,0,2:T(8,128)(2,1)}), bf16[2,8,256,256]{3,1,0,2:T(8,128)(2,1)S(1)}, u32[]{:S(2)}, u32[]{:S(2)}) %all-to-all-start) | async-done | bytes 2097184 | tf_op jit(solution)/shard_map/all_to_all | solution.py:79
  321.3 0.7 copy.19
  322.0 3.0 fusion.2
  325.0 3.3 copy.21
  328.3 54.7 %all_to_all.33 = bf16[16,256,256]{2,0,1:T(8,128)(2,1)S(1)} all-to-all(bf16[16,256,256]{2,0,1:T(8,128)(2,1)S(1)} %copy.21), channel_id=1, replica_groups=mesh['rx'=32,'freq'=16] {'freq'}, dimensions={1} | all-to-all | bytes 4194304 | tf_op jit(solution)/shard_map/all_to_all | solution.py:81
  383.1 2.2 copy.23
  (6 shorter events, 0.1 us)
Async XLA Ops:
  6.5 9.8 %copy-start = (bf16[2,8,32,256]{3,2,1,0:T(8,128)(2,1)S(1)}, bf16[2,8,32,256]{3,2,1,0:T(8,128)(2,1)}, u32[]{:S(2)}) copy-start(bf16[2,8,32,256]{3,2,1,0:T(8,128)(2,1)} %param.2) | copy-start | bytes 786436
  6.5 248.3 %all-reduce.2.cloned.1.call-start = ((), (), s32[]{:S(2)}) async-start(), calls=%async_computation.2 | async-start | bytes 524288 | tf_op jit(solution)/shard_map/psum | solution.py:31
  7.7 6.0 %collective-permute-start = (f32[1,32,256]{2,1,0:T(8,128)S(1)}, f32[1,32,256]{2,1,0:T(8,128)S(1)}, u32[]{:S(2)}, u32[]{:S(2)}) collective-permute-start(f32[1,32,256]{2,1,0:T(8,128)S(1)} %get-tuple-element.11), channel_id=1, source_target_pairs={{0,1},{1,2},{2,3},{3,4},{4,5},{5,6},{6,7},{7,8},{8,9},{9,10},{10,1... | collective-permute-start | bytes 98312 | tf_op jit(solution)/shard_map/ppermute | solution.py:20
  11.7 4.7 %collective-permute-start.1 = (f32[1,32,256]{2,1,0:T(8,128)S(1)}, f32[1,32,256]{2,1,0:T(8,128)S(1)}, u32[]{:S(2)}, u32[]{:S(2)}) collective-permute-start(f32[1,32,256]{2,1,0:T(8,128)S(1)} %get-tuple-element.12), channel_id=1, source_target_pairs={{1,0},{2,1},{3,2},{4,3},{5,4},{6,5},{7,6},{8,7},{9,8},{10,9},{11,1... | collective-permute-start | bytes 98312 | tf_op jit(solution)/shard_map/ppermute | solution.py:22
  259.8 61.5 %all-to-all-start = ((bf16[2,8,256,256]{3,1,0,2:T(8,128)(2,1)}), bf16[2,8,256,256]{3,1,0,2:T(8,128)(2,1)S(1)}, u32[]{:S(2)}, u32[]{:S(2)}) async-start(bf16[2,8,256,256]{3,1,0,2:T(8,128)(2,1)} %copy.17), calls=%async_computation | async-start | bytes 4194304 | tf_op jit(solution)/shard_map/all_to_all | solution.py:79
Sparse Core Ops, SparseCore 0:
  17.4 237.4 all-reduce.1
where the time goes:
time: 392 us
  waiting for transfers between devices  293 us (75%)
  blocking collectives  54.7 us (14%)
  between operations  14.2 us (4%)
  starting transfers between devices  13.3 us (3%)
  local copies, waits for them, and re-layouts  9.73 us (2%)
  matrix products  4 us (1%)
    psum x1, waiting for transfers between devices, broadcast(): return lax.psum(kept, axis)  238 us
    all_to_all x1, blocking collectives, on_device(): lax.all_to_all(lagged, 'freq', split_axis=1, concat_axis=0, tiled=True)  54.7 us
    all_to_all x1, waiting for transfers between devices, on_device(): lax.all_to_all(cross, 'freq', split_axis=2, concat_axis=1, tiled=True)  52.8 us
    all_to_all x1, starting transfers between devices, on_device(): lax.all_to_all(cross, 'freq', split_axis=2, concat_axis=1, tiled=True)  8.08 us
  transfers between devices with their start and end apart: 4, of which 3 were waited for; matrix products, arithmetic and copies ran while one was open for 0% of the time, Pallas kernels for 0%

commit v1 on v0

--- a/solution.py
+++ b/solution.py
@@ -3,6 +3,7 @@
 import jax.numpy as jnp
 from jax import lax
 from jax.sharding import PartitionSpec as P
+from jax.lax import all_gather
 
 F = 128
 W = 32
@@ -28,7 +29,11 @@
 
 def broadcast(value, axis, source):
     kept = jnp.where(lax.axis_index(axis) == source, value, 0).astype(value.dtype)
-    return lax.psum(kept, axis)
+
+    def manage_notes_over_axis(mat):
+        return jnp.sum(all_gather(mat, axis_name=axis), axis=0)
+
+    return manage_notes_over_axis(kept)
 
 
 def whiten(planes_in):

time: 392 us -> 246 us (0.63)
  waiting for transfers between devices: 293 us -> 140 us
  other arithmetic: 3.15 us -> 8.71 us
    psum x1 -> x0, waiting for transfers between devices: 238 us -> none  [broadcast(): return lax.psum(kept, axis)]
    all_gather x0 -> x1, waiting for transfers between devices: none -> 85.4 us  [manage_notes_over_axis(): return jnp.sum(all_gather(mat, axis_name=axis), axis=0)]
    reduce_sum x0 -> x1, other arithmetic: none -> 5.56 us  [manage_notes_over_axis(): return jnp.sum(all_gather(mat, axis_name=axis), axis=0)]
where the time goes in v1:
time: 246 us
  waiting for transfers between devices  140 us (57%)
  blocking collectives  55.6 us (23%)
  starting transfers between devices  14.2 us (6%)
  between operations  14.2 us (6%)
  local copies, waits for them, and re-layouts  8.76 us (4%)
  other arithmetic  8.71 us (4%)
  matrix products  4.01 us (2%)
    all_gather x1, waiting for transfers between devices, manage_notes_over_axis(): return jnp.sum(all_gather(mat, axis_name=axis), axis=0)  85.4 us
    all_to_all x1, blocking collectives, on_device(): lax.all_to_all(lagged, 'freq', split_axis=1, concat_axis=0, tiled=True)  55.6 us
    all_to_all x1, waiting for transfers between devices, on_device(): lax.all_to_all(cross, 'freq', split_axis=2, concat_axis=1, tiled=True)  52.1 us
    all_to_all x1, starting transfers between devices, on_device(): lax.all_to_all(cross, 'freq', split_axis=2, concat_axis=1, tiled=True)  8.97 us
    reduce_sum x1, other arithmetic, manage_notes_over_axis(): return jnp.sum(all_gather(mat, axis_name=axis), axis=0)  5.56 us
  transfers between devices with their start and end apart: 4, of which 3 were waited for; matrix products, arithmetic and copies ran while one was open for 0% of the time, Pallas kernels for 0%

profile of v1, /device:TPU:1, one launch (start us, length us, event | category | flops | bytes accessed | tf_op | source)
XLA Modules:
  0.0 245.5 jit_solution(8558948940073464919)
XLA Ops:
  6.5 0.0 all-gather.3.cloned.1.call-start
  6.5 1.1 convert_element_type.25
  7.6 0.1 fusion.10
  7.7 3.9 %collective-permute-start = (f32[1,32,256]{2,1,0:T(8,128)S(1)}, f32[1,32,256]{2,1,0:T(8,128)S(1)}, u32[]{:S(2)}, u32[]{:S(2)}) collective-permute-start(f32[1,32,256]{2,1,0:T(8,128)S(1)} %get-tuple-element.11), channel_id=1, source_target_pairs={{0,1},{1,2},{2,3},{3,4},{4,5},{5,6},{6,7},{7,8},{8,9},{9,10},{10,1... | collective-permute-start | bytes 98312 | tf_op jit(solution)/shard_map/ppermute | solution.py:21
  11.7 1.3 collective-permute-start.1
  13.0 0.1 fusion.29
  13.7 0.0 collective-permute-done
  13.7 2.6 %collective-permute-done.1 = f32[1,32,256]{2,1,0:T(8,128)S(1)} collective-permute-done((f32[1,32,256]{2,1,0:T(8,128)S(1)}, f32[1,32,256]{2,1,0:T(8,128)S(1)}, u32[]{:S(2)}, u32[]{:S(2)}) %collective-permute-start.1) | collective-permute-done | bytes 32800 | tf_op jit(solution)/shard_map/ppermute | solution.py:23
  16.4 0.8 broadcast_select_fusion
  17.2 0.0 all-gather.3.cloned.1.call-update
  17.3 85.4 %all-gather.3.cloned.1.call-done = bf16[64,8,32,256]{3,2,1,0:T(8,128)(2,1)} async-done(((bf16[2,8,32,256]{3,2,1,0:T(8,128)(2,1)}), bf16[64,8,32,256]{3,2,1,0:T(8,128)(2,1)}) %all-gather.3.cloned.1.call-update) | async-done | bytes 8388624 | tf_op jit(solution)/shard_map/all_gather | solution.py:34
  102.6 5.6 %reduce_sum.12 = bf16[2,8,32,256]{3,2,1,0:T(8,128)(2,1)S(1)} reduce(bf16[32,2,8,32,256]{4,3,2,1,0:T(8,128)(2,1)} %bitcast.36, bf16[]{:T(256)} %constant.31.clone.1), dimensions={0}, to_apply=%region_0.1 | reduce | flops 4063232 | bytes 8650754 | tf_op jit(solution)/shard_map/reduce_sum | solution.py:34
  108.2 0.5 convolution_bitcast_fusion.1
  108.7 0.5 convolution_bitcast_fusion
  109.2 0.5 fusion
  109.7 2.5 %copy.17 = bf16[2,8,256,256]{3,1,0,2:T(8,128)(2,1)} copy(bf16[2,8,256,256]{3,2,1,0:T(8,128)(2,1)S(1)} %fusion) | data formatting | bytes 4194304 | tf_op jit(solution)/shard_map/convert_element_type | solution.py:82
  112.2 9.0 %all-to-all-start = ((bf16[2,8,256,256]{3,1,0,2:T(8,128)(2,1)}), bf16[2,8,256,256]{3,1,0,2:T(8,128)(2,1)S(1)}, u32[]{:S(2)}, u32[]{:S(2)}) async-start(bf16[2,8,256,256]{3,1,0,2:T(8,128)(2,1)} %copy.17), calls=%async_computation | async-start | bytes 4194304 | tf_op jit(solution)/shard_map/all_to_all | solution.py:84
  121.2 0.5 negate_convert_fusion
  121.7 52.1 %all-to-all-done = bf16[2,8,256,256]{3,1,0,2:T(8,128)(2,1)S(1)} async-done(((bf16[2,8,256,256]{3,1,0,2:T(8,128)(2,1)}), bf16[2,8,256,256]{3,1,0,2:T(8,128)(2,1)S(1)}, u32[]{:S(2)}, u32[]{:S(2)}) %all-to-all-start) | async-done | bytes 2097184 | tf_op jit(solution)/shard_map/all_to_all | solution.py:84
  173.8 0.7 copy.19
  174.5 3.0 %fusion.2 = bf16[16,256,256]{1,2,0:T(8,128)(2,1)} fusion(bf16[256,16,256]{2,1,0:T(8,128)(2,1)S(1)} %bitcast.39, bf16[128,256]{1,0:T(8,128)(2,1)S(1)} %get-tuple-element.13, bf16[128,256]{1,0:T(8,128)(2,1)S(1)} %get-tuple-element.14), kind=kOutput, calls=%fused_computation.4 | convolution fusion | flops 539230208 | bytes 4325376 | tf_op jit(solution)/shard_map/kl,ksr->slr/dot_general | solution.py:71
  177.5 3.3 %copy.21 = bf16[16,256,256]{2,0,1:T(8,128)(2,1)S(1)} copy(bf16[16,256,256]{1,2,0:T(8,128)(2,1)} %fusion.2) | data formatting | bytes 4194304 | tf_op jit(solution)/shard_map/convert_element_type | solution.py:74
  180.9 55.6 %all_to_all.33 = bf16[16,256,256]{2,0,1:T(8,128)(2,1)S(1)} all-to-all(bf16[16,256,256]{2,0,1:T(8,128)(2,1)S(1)} %copy.21), channel_id=1, replica_groups=mesh['rx'=32,'freq'=16] {'freq'}, dimensions={1} | all-to-all | bytes 4194304 | tf_op jit(solution)/shard_map/all_to_all | solution.py:86
  236.5 2.2 copy.23
  (7 shorter events, 0.1 us)
Async XLA Ops:
  6.5 9.8 %copy-start = (bf16[2,8,32,256]{3,2,1,0:T(8,128)(2,1)S(1)}, bf16[2,8,32,256]{3,2,1,0:T(8,128)(2,1)}, u32[]{:S(2)}) copy-start(bf16[2,8,32,256]{3,2,1,0:T(8,128)(2,1)} %param.2) | copy-start | bytes 786436
  6.5 96.1 %all-gather.3.cloned.1.call-start = ((), (), s32[]{:S(2)}) async-start(), calls=%async_computation.2 | async-start | bytes 8650752 | tf_op jit(solution)/shard_map/all_gather | solution.py:34
  7.7 6.0 %collective-permute-start = (f32[1,32,256]{2,1,0:T(8,128)S(1)}, f32[1,32,256]{2,1,0:T(8,128)S(1)}, u32[]{:S(2)}, u32[]{:S(2)}) collective-permute-start(f32[1,32,256]{2,1,0:T(8,128)S(1)} %get-tuple-element.11), channel_id=1, source_target_pairs={{0,1},{1,2},{2,3},{3,4},{4,5},{5,6},{6,7},{7,8},{8,9},{9,10},{10,1... | collective-permute-start | bytes 98312 | tf_op jit(solution)/shard_map/ppermute | solution.py:21
  11.7 4.7 %collective-permute-start.1 = (f32[1,32,256]{2,1,0:T(8,128)S(1)}, f32[1,32,256]{2,1,0:T(8,128)S(1)}, u32[]{:S(2)}, u32[]{:S(2)}) collective-permute-start(f32[1,32,256]{2,1,0:T(8,128)S(1)} %get-tuple-element.12), channel_id=1, source_target_pairs={{1,0},{2,1},{3,2},{4,3},{5,4},{6,5},{7,6},{8,7},{9,8},{10,9},{11,1... | collective-permute-start | bytes 98312 | tf_op jit(solution)/shard_map/ppermute | solution.py:23
  112.2 61.6 %all-to-all-start = ((bf16[2,8,256,256]{3,1,0,2:T(8,128)(2,1)}), bf16[2,8,256,256]{3,1,0,2:T(8,128)(2,1)S(1)}, u32[]{:S(2)}, u32[]{:S(2)}) async-start(bf16[2,8,256,256]{3,1,0,2:T(8,128)(2,1)} %copy.17), calls=%async_computation | async-start | bytes 4194304 | tf_op jit(solution)/shard_map/all_to_all | solution.py:84
Sparse Core Ops, SparseCore 0:
  17.4 85.2 all-gather.2
